TPU v7x, 32 devices: a whole 2x2x4 slice. The times are simulated.
32 devices in a mesh: row: 4 (over y, x), col: 8 (over z, core).
Axes of the slice: x: 2, y: 2, z: 4, core: 2. Of those that a mesh axis runs over, the one named last changes fastest.
Arguments:
- amplitudes: float32 [8, 24, 1, 128, 128], P('col', 'row'), may hold values from -6 to 6
- integrals: float32 [2, 512, 4096], P(None, 'row', 'col'), may hold values from -0.5 to 0.5
- owner_column: int32 [2], replicated, may hold values from 0 to 7
- occ_irrep: int32 [24], replicated, may hold values from 0 to 7, as said below
- pair_irrep: int32 [2, 4], replicated, may hold values from 0 to 7, as said below
Outputs:
- ladder: float32 [3072, 4096], P('row', 'col')
Inputs may be any that keep to these rules, and one draw needn't show every extreme that they name: `occ_irrep`: every irrep 0 to 7 labels some occupied-pair tile. `pair_irrep`: in each section no irrep labels more than 1 of the 4 panel tiles, and some irrep labels exactly 1.
All inputs are finite; a program needn't handle non-finite values.
Results may differ from a plain program's by a relative error of at most 0.0001.
Values sent between devices are 32-bit elements; how exact they have to be, the bound alone decides.
No kernel may reach another device: no remote copies, remote signals or barrier semaphores. Data moves between devices by JAX's collectives and lax.ppermute only.
A program may use at most 64 MiB of HBM per device.

v0:
```python
import jax
import jax.numpy as jnp
from jax import lax
from jax.sharding import PartitionSpec as P


def spread(value, axis, source):
    kept = jnp.where(lax.axis_index(axis) == source, value, 0).astype(value.dtype)
    return lax.psum(kept, axis)


def slot_tables(occ_labels, pair_labels, slot_count):
    matches = occ_labels[:, None] == pair_labels[None, :]
    order_rank = jnp.cumsum(matches.astype(jnp.int32), axis=1) - 1
    slot_ids = jnp.arange(slot_count, dtype=jnp.int32)
    chosen = matches[:, None, :] & (order_rank[:, None, :] == slot_ids[None, :, None])
    positions = jnp.arange(pair_labels.shape[0], dtype=jnp.int32)
    tile_index = jnp.sum(chosen.astype(jnp.int32) * positions[None, None, :], axis=2)
    valid_slot = jnp.any(chosen, axis=2)
    return (tile_index, valid_slot, chosen)


def on_device(amplitudes, integrals, owner_column, occ_irrep, pair_irrep):
    tiles_here = amplitudes.shape[1]
    slot_count = amplitudes.shape[2]
    tile_size = amplitudes.shape[3]
    section_count = integrals.shape[0]
    columns = integrals.shape[2]
    first_tile = lax.axis_index("row") * tiles_here
    occ_mine = lax.dynamic_slice_in_dim(occ_irrep, first_tile, tiles_here)

    def fetch_panel(which_section):
        return spread(amplitudes[0], "col", owner_column[which_section])

    tables = [
        slot_tables(occ_mine, pair_irrep[which_section], slot_count)
        for which_section in range(section_count)
    ]
    panels = [fetch_panel(which_section) for which_section in range(section_count)]
    section_rows = [
        lax.all_gather(integrals[which_section], "row", axis=0, tiled=True)
        for which_section in range(section_count)
    ]
    running = jnp.zeros((tiles_here, tile_size, columns), jnp.float32)
    for which_section in range(section_count):
        tile_index, valid_slot, chosen = tables[which_section]
        amp_panel = panels[which_section] * valid_slot[:, :, None, None].astype(jnp.float32)
        row_tiles = section_rows[which_section].reshape(-1, tile_size, columns)
        picked = jnp.take(row_tiles, tile_index, axis=0)
        running = running + jnp.einsum(
            "osij,osjv->oiv", amp_panel, picked, precision=lax.Precision.HIGHEST
        )
    return running.reshape(tiles_here * tile_size, columns)


def solution(mesh):
    return jax.shard_map(
        on_device,
        mesh=mesh,
        in_specs=(P("col", "row", None, None, None), P(None, "row", "col"), P(), P(), P()),
        out_specs=P("row", "col"),
        check_vma=False,
    )
```

profile of v0, /device:TPU:0, one launch (start us, length us, event | category | flops | bytes accessed | tf_op | source)
XLA Modules:
  0.0 86.2 jit_solution(2370965380139020534)
XLA Ops:
  7.4 0.0 copy-start.2
  7.4 0.0 copy-start
  7.4 0.0 copy-start.3
  7.4 0.0 copy-start.4
  7.4 0.0 all-gather.7.cloned.1.call-start
  7.4 1.9 %fusion.25 = (f32[1,128,512]{2,1,0:T(8,128)}, f32[1,128,512]{2,1,0:T(8,128)}) fusion(f32[2,128,512]{2,1,0:T(8,128)} %param.8), kind=kLoop, calls=%fused_computation.45 | loop fusion | bytes 1048576 | tf_op jit(solution)/shard_map/slice | solution.py:41
  9.3 0.0 all-gather.7.cloned.1.call-update
  9.3 0.0 all-gather.5.cloned.1.call-start
  9.4 0.7 all-gather.5.cloned.1.call-update
  10.1 0.0 all-reduce.3.cloned.1.call-start
  10.2 0.0 copy-done.2
  10.2 0.6 fusion.26
  12.0 0.0 copy-done
  12.0 1.0 %select_bitcast_fusion.1 = (f32[6,1,128,128]{3,2,0,1:T(8,128)}, f32[6,1,128,128]{3,2,0,1:T(8,128)}) fusion(f32[1,6,1,128,128]{4,3,2,1,0:T(8,128)S(1)} %copy-done, pred[]{:T(512)S(6)} %eq.98, pred[]{:T(512)S(6)} %eq.107), kind=kLoop, calls=%fused_computation.18 | loop fusion | flops 196608 | bytes 1179650 | tf_op jit(solution)/shard_map/jit(_where)/select_n | solution.py:8
  13.0 0.0 all-reduce.3.cloned.1.call-update
  13.0 0.0 copy-done.3
  13.1 0.0 copy-done.4
  13.1 0.1 dynamic_slice.3
  13.1 0.1 compare_convert_fusion.1
  13.3 0.1 fusion.23
  13.5 25.9 %all-gather.7.cloned.1.call-done = f32[1,512,512]{2,1,0:T(8,128)} async-done(((f32[1,128,512]{2,1,0:T(8,128)}), f32[1,512,512]{2,1,0:T(8,128)}) %all-gather.7.cloned.1.call-update) | async-done | bytes 1048592 | tf_op jit(solution)/shard_map/all_gather | solution.py:41
  39.4 1.9 %gather_fusion.1 = f32[6,128,512]{2,1,0:T(8,128)S(1)} fusion(f32[4,128,512]{2,1,0:T(8,128)} %bitcast.69, s32[1024]{0:T(1024)S(1)} %pad_clamp_fusion), kind=kCustom, calls=%fused_computation.1.clone | custom fusion | bytes 3145752 | tf_op jit(solution)/shard_map/jit(_take)/gather | solution.py:49
  41.3 26.8 %all-gather.5.cloned.1.call-done = f32[1,512,512]{2,1,0:T(8,128)} async-done(((f32[1,128,512]{2,1,0:T(8,128)}), f32[1,512,512]{2,1,0:T(8,128)}) %all-gather.5.cloned.1.call-update) | async-done | bytes 1048592 | tf_op jit(solution)/shard_map/all_gather | solution.py:41
  68.1 1.9 %gather_fusion = f32[6,128,512]{2,1,0:T(8,128)S(1)} fusion(f32[4,128,512]{2,1,0:T(8,128)} %bitcast.70, s32[1024]{0:T(1024)S(1)} %pad_clamp_fusion.1), kind=kCustom, calls=%fused_computation.clone | custom fusion | bytes 3145752 | tf_op jit(solution)/shard_map/jit(_take)/gather | solution.py:49
  70.0 3.4 %all-reduce.3.cloned.1.call-done = (f32[6,1,128,128]{3,2,0,1:T(8,128)}, f32[6,1,128,128]{3,2,0,1:T(8,128)}) async-done(((f32[6,1,128,128]{3,2,0,1:T(8,128)}, f32[6,1,128,128]{3,2,0,1:T(8,128)}), (f32[6,1,128,128]{3,2,0,1:T(8,128)}, f32[6,1,128,128]{3,2,0,1:T(8,128)})) %all-reduce.3.cloned.1.call-update) | async-done | bytes 786448 | tf_op jit(solution)/shard_map/psum | solution.py:9
  73.4 0.0 copy-start.1
  73.4 2.6 %fusion = f32[6,128,512]{2,1,0:T(8,128)S(1)} fusion(f32[6,128,512]{2,1,0:T(8,128)S(1)} %gather_fusion.1, pred[6]{0:T(512)(128)(4,1)S(1)} %and_bitcast_fusion, f32[6,1,128,128]{3,2,0,1:T(8,128)} %get-tuple-element.6, f32[6]{0:T(128)S(1)} %convert_element_type.30), kind=kOutput, calls=%fused_computation.2 | convolution fusion | flops 604471296 | bytes 3538974 | tf_op jit(solution)/shard_map/osij,osjv->oiv/dot_general | solution.py:50
  76.0 0.0 copy-done.1
  76.0 2.7 %fusion.4 = f32[6,128,512]{2,1,0:T(8,128)} fusion(f32[6,128,512]{2,1,0:T(8,128)S(1)} %fusion, f32[6,128,512]{2,1,0:T(8,128)S(1)} %gather_fusion, pred[6]{0:T(512)(128)(4,1)S(1)} %and_bitcast_fusion.1, f32[6,1,128,128]{3,2,0,1:T(8,128)S(1)} %copy-done.1, f32[6]{0:T(128)S(1)} %convert_element_type.28), kind=kOutput, calls=%fused_computation.8 | convolution fusion | flops 604864512 | bytes 5111838 | tf_op jit(solution)/shard_map/osij,osjv->oiv/dot_general | solution.py:50
  (13 shorter events, 0.2 us)
Async XLA Ops:
  7.4 2.8 %copy-start.2 = (s32[2]{0:T(128)S(1)}, s32[2]{0:T(128)}, u32[]{:S(2)}) copy-start(s32[2]{0:T(128)} %param.9) | copy-start | bytes 28
  7.4 4.7 %copy-start = (f32[1,6,1,128,128]{4,3,2,1,0:T(8,128)S(1)}, f32[1,6,1,128,128]{4,3,2,1,0:T(8,128)}, u32[]{:S(2)}) copy-start(f32[1,6,1,128,128]{4,3,2,1,0:T(8,128)} %param.7) | copy-start | bytes 1179652
  7.4 5.7 %copy-start.3 = (s32[2,4]{1,0:T(2,128)S(1)}, s32[2,4]{1,0:T(2,128)}, u32[]{:S(2)}) copy-start(s32[2,4]{1,0:T(2,128)} %param.11) | copy-start | bytes 100
  7.4 5.7 %copy-start.4 = (s32[24]{0:T(128)S(1)}, s32[24]{0:T(128)}, u32[]{:S(2)}) copy-start(s32[24]{0:T(128)} %param.10) | copy-start | bytes 292
  7.4 32.1 %all-gather.7.cloned.1.call-start = ((), (), s32[]{:S(2)}) async-start(), calls=%async_computation.1 | async-start | bytes 1310720 | tf_op jit(solution)/shard_map/all_gather | solution.py:41
  9.3 58.7 %all-gather.5.cloned.1.call-start = ((), (), s32[]{:S(2)}) async-start(), calls=%async_computation | async-start | bytes 1310720 | tf_op jit(solution)/shard_map/all_gather | solution.py:41
  10.1 63.3 %all-reduce.3.cloned.1.call-start = ((), (), s32[]{:S(2)}) async-start(), calls=%async_computation.2 | async-start | bytes 1572864 | tf_op jit(solution)/shard_map/psum | solution.py:9
  73.4 2.6 %copy-start.1 = (f32[6,1,128,128]{3,2,0,1:T(8,128)S(1)}, f32[6,1,128,128]{3,2,0,1:T(8,128)}, u32[]{:S(2)}) copy-start(f32[6,1,128,128]{3,2,0,1:T(8,128)} %get-tuple-element.7) | copy-start | bytes 1179652
Sparse Core Ops, SparseCore 0:
  10.0 29.3 all-gather.6
  41.4 26.6 all-gather.4
Sparse Core Ops, SparseCore 1:
  13.1 60.2 all-reduce.2
where the time goes:
time: 86.4 us; the launch traced here: 86.2 us
  waiting for transfers between devices  56.8 us (66%)
  between operations  16.2 us (19%)
  local copies, waits for them, and re-layouts  6.36 us (7%)
  matrix products  5.32 us (6%)
  other arithmetic  1.29 us (1%)
    all_gather x2, waiting for transfers between devices, on_device(): lax.all_gather(integrals[which_section], 'row', axis=0, tiled=True)  52.7 us
    dot_general x2, matrix products, on_device(): jnp.einsum('osij,osjv->oiv', amp_panel, picked, precision=lax.Precision.H...  5.32 us
    gather x2, local copies, waits for them, and re-layouts, on_device(): picked = jnp.take(row_tiles, tile_index, axis=0)  3.76 us
    psum x1, waiting for transfers between devices, spread(): return lax.psum(kept, axis)  3.43 us
    slice x1, local copies, waits for them, and re-layouts, on_device(): integrals[which_section]  1.9 us
  transfers between devices with their start and end apart: 3, of which 3 were waited for; matrix products, arithmetic and copies ran while one was open for 7% of the time, Pallas kernels for 0%

commit v1 on v0

v1 whole, which is shorter than its diff:
```python
import functools

import jax
import jax.numpy as jnp
from jax import lax
from jax.experimental import pallas as pl
from jax.experimental.pallas import tpu as pltpu
from jax.sharding import PartitionSpec as P


def bits_of(count):
    assert count & (count - 1) == 0
    return [1 << place for place in range(count.bit_length() - 1)]


def swap(value, axis, size, bit):
    return lax.ppermute(value, axis, [(i, i ^ bit) for i in range(size)])


def gather_rows(block, row_size, order):
    held = {0: block}
    for bit in order:
        for offset in list(held):
            held[offset | bit] = swap(held[offset], "row", row_size, bit)
    return [held[offset] for offset in range(row_size)]


def halves(value, upper):
    middle = value.shape[1] // 2
    low, high = value[:, :middle], value[:, middle:]
    return jnp.where(upper, high, low), jnp.where(upper, low, high)


def fetch_panels(panel, owners, col_size):
    bits = bits_of(col_size)
    me = lax.axis_index("col")
    values = [panel] * len(owners)
    for bit in bits[:-1]:
        upper = (me & bit) != 0
        if bit == bits[0]:
            kept, given = halves(panel, upper)
            arrived = swap(given, "col", col_size, bit)
            pairs = [(kept, arrived)] * len(owners)
        else:
            parts = [halves(value, upper) for value in values]
            pairs = [(kept, swap(given, "col", col_size, bit)) for kept, given in parts]
        values = [
            jnp.where((owner & bit) == (me & bit), kept, arrived)
            for owner, (kept, arrived) in zip(owners, pairs)
        ]
    last = bits[-1]
    values = [
        jnp.where((owner & last) == (me & last), value, swap(value, "col", col_size, last))
        for owner, value in zip(owners, values)
    ]
    panels = []
    for value in values:
        held = {0: value}
        for place, bit in reversed(list(enumerate(bits[:-1]))):
            for offset in list(held):
                step = 1 << (len(bits) - 2 - place)
                held[offset | step] = swap(held[offset], "col", col_size, bit)
        panels.append([held[offset] for offset in range(len(held))])
    return panels


def piece_number(col_size):
    me = lax.axis_index("col")
    number = jnp.int32(0)
    for bit in bits_of(col_size)[:-1]:
        number = 2 * number + jnp.where((me & bit) != 0, 1, 0)
    return number


def slot_tables(occ_labels, pair_labels, slot_count):
    matches = occ_labels[:, None] == pair_labels[None, :]
    order_rank = jnp.cumsum(matches.astype(jnp.int32), axis=1) - 1
    slot_ids = jnp.arange(slot_count, dtype=jnp.int32)
    chosen = matches[:, None, :] & (order_rank[:, None, :] == slot_ids[None, :, None])
    positions = jnp.arange(pair_labels.shape[0], dtype=jnp.int32)
    tile_index = jnp.sum(chosen.astype(jnp.int32) * positions[None, None, :], axis=2)
    return tile_index, jnp.any(chosen, axis=2).astype(jnp.int32)


def split(value):
    high = value.astype(jnp.bfloat16)
    return high, (value - high.astype(jnp.float32)).astype(jnp.bfloat16)


def products_kernel(sections, slots, pieces, blocks, tiles, tile, columns, *refs):
    source_ref, valid_ref, piece_ref = refs[:3]
    piece_refs = refs[3 : 3 + sections * pieces]
    block_refs = refs[3 + sections * pieces : 3 + sections * (pieces + blocks)]
    out_ref, rows_high, rows_low, amp, result, sems = refs[3 + sections * (pieces + blocks) :]
    length = tile // pieces
    for k in range(sections):
        for i in range(pieces):
            start = pl.multiple_of((piece_ref[0] ^ i) * length, length)
            for o in range(tiles):
                for s in range(slots):
                    valid = valid_ref[k, o, s] != 0
                    value = jnp.where(valid, piece_refs[k * pieces + i][o, :, s * tile : (s + 1) * tile], 0.0)
                    amp[o, pl.ds(start, length), pl.ds((k * slots + s) * tile, tile)] = value
        for i in range(blocks):
            high, low = split(block_refs[k * blocks + i][...])
            rows_high[k, i] = high
            rows_low[k, i] = low

    def copy(o):
        return pltpu.make_async_copy(result.at[o], out_ref.at[pl.ds(o * tile, tile)], sems.at[o])

    for o in range(tiles):
        places = [(k, source_ref[k, o, s]) for k in range(sections) for s in range(slots)]
        high = jnp.concatenate([rows_high[k, i] for k, i in places], axis=0)
        low = jnp.concatenate([rows_low[k, i] for k, i in places], axis=0)
        dot = functools.partial(jnp.dot, preferred_element_type=jnp.float32)
        amp_high, amp_low = split(amp[o])
        result[o] = dot(amp_high, high) + (dot(amp_high, low) + dot(amp_low, high))
        copy(o).start()
    for o in range(tiles):
        copy(o).wait()


def products(source, valid, piece, panels, blocks, tiles, slots, tile):
    sections, columns = len(panels), blocks[0][0].shape[1]
    pieces, count = len(panels[0]), len(blocks[0])
    depth = sections * slots * tile
    smem = pl.BlockSpec(memory_space=pltpu.SMEM)
    vmem = pl.BlockSpec(memory_space=pltpu.VMEM)
    flat = [p for section in panels for p in section] + [b for section in blocks for b in section]
    return pl.pallas_call(
        functools.partial(products_kernel, sections, slots, pieces, count, tiles, tile, columns),
        out_shape=jax.ShapeDtypeStruct((tiles * tile, columns), jnp.float32),
        in_specs=[smem] * 3 + [vmem] * len(flat),
        out_specs=pl.BlockSpec(memory_space=pl.ANY),
        scratch_shapes=[
            pltpu.VMEM((sections, count, tile, columns), jnp.bfloat16),
            pltpu.VMEM((sections, count, tile, columns), jnp.bfloat16),
            pltpu.VMEM((tiles, tile, depth), jnp.float32),
            pltpu.VMEM((tiles, tile, columns), jnp.float32),
            pltpu.SemaphoreType.DMA((tiles,)),
        ],
        compiler_params=pltpu.CompilerParams(vmem_limit_bytes=40 * 1024 * 1024),
        cost_estimate=pl.CostEstimate(
            flops=6 * tiles * tile * depth * columns, bytes_accessed=4 * tiles * tile * columns, transcendentals=0
        ),
    )(source, valid, piece, *flat)


def on_device(row_size, col_size, amplitudes, integrals, owner_column, occ_irrep, pair_irrep):
    tiles, slots, tile = amplitudes.shape[1:4]
    sections = integrals.shape[0]
    me = lax.axis_index("row")
    occ_mine = lax.dynamic_slice_in_dim(occ_irrep, me * tiles, tiles)
    tables = [slot_tables(occ_mine, pair_irrep[k], slots) for k in range(sections)]
    source = jnp.stack([index ^ me for index, _ in tables])
    valid = jnp.stack([valid for _, valid in tables])

    order = bits_of(row_size)
    blocks = [
        gather_rows(integrals[k], row_size, order[::-1] if k % 2 == 0 else order) for k in range(sections)
    ]
    panel = amplitudes[0].transpose(0, 2, 1, 3).reshape(tiles, tile, slots * tile)
    panels = fetch_panels(panel, [owner_column[k] for k in range(sections)], col_size)
    piece = piece_number(col_size).reshape(1)
    return products(source, valid, piece, panels, blocks, tiles, slots, tile)


def solution(mesh):
    return jax.shard_map(
        functools.partial(on_device, mesh.shape["row"], mesh.shape["col"]),
        mesh=mesh,
        in_specs=(P("col", "row", None, None, None), P(None, "row", "col"), P(), P(), P()),
        out_specs=P("row", "col"),
        check_vma=False,
    )
```

time: 86.4 us -> 47.1 us (0.55)
  waiting for transfers between devices: 56.8 us -> 19.8 us
  starting transfers between devices: 0.12 us -> 16.5 us
  between operations: 16.2 us -> 4.06 us
  matrix products: 5.32 us -> 0 us
  local copies, waits for them, and re-layouts: 6.36 us -> 2.2 us
  Pallas kernels: 0 us -> 2.85 us
    all_gather x2 -> x0, waiting for transfers between devices: 52.7 us -> none  [on_device(): lax.all_gather(integrals[which_section], 'row', axis=0, tiled=True)]
    ppermute x0 -> x17, waiting for transfers between devices: none -> 19.8 us  [swap(): return lax.ppermute(value, axis, [(i, i ^ bit) for i in range(size)])]
    ppermute x0 -> x17, starting transfers between devices: none -> 16.5 us  [swap(): return lax.ppermute(value, axis, [(i, i ^ bit) for i in range(size)])]
    dot_general x2 -> x0, matrix products: 5.32 us -> none  [on_device(): jnp.einsum('osij,osjv->oiv', amp_panel, picked, precision=lax.Precision.H...]
    gather x2 -> x0, local copies, waits for them, and re-layouts: 3.76 us -> none  [on_device(): picked = jnp.take(row_tiles, tile_index, axis=0)]
    psum x1 -> x0, waiting for transfers between devices: 3.43 us -> none  [spread(): return lax.psum(kept, axis)]
    pallas_call x0 -> x1, Pallas kernels: none -> 2.85 us  [products(): pl.pallas_call(functools.partial(products_kernel, sections, slots, pieces...]
    slice x3 -> x2, local copies, waits for them, and re-layouts: 2.5 us -> 0.59 us  [the longest x1 0.58 us: on_device(): owner_column[k]]
  transfers between devices with their start and end apart: 3 -> 17, of which waited for: 3 -> 7; matrix products, arithmetic and copies ran while one was open for 7% -> 5% of each run, Pallas kernels for 0% -> 0%
where the time goes in v1:
time: 47.1 us; the launch traced here: 46.9 us
  waiting for transfers between devices  19.8 us (42%)
  starting transfers between devices  16.5 us (35%)
  between operations  4.06 us (9%)
  Pallas kernels  2.85 us (6%)
  local copies, waits for them, and re-layouts  2.2 us (5%)
  other arithmetic  1.48 us (3%)
    ppermute x17, waiting for transfers between devices, swap(): return lax.ppermute(value, axis, [(i, i ^ bit) for i in range(size)])  19.8 us
    ppermute x17, starting transfers between devices, swap(): return lax.ppermute(value, axis, [(i, i ^ bit) for i in range(size)])  16.5 us
    pallas_call x1, Pallas kernels, products(): pl.pallas_call(functools.partial(products_kernel, sections, slots, pieces...  2.85 us
    squeeze x1, local copies, waits for them, and re-layouts, on_device(): integrals[k]  1.11 us
    select_n x3, other arithmetic, halves(): return (jnp.where(upper, high, low), jnp.where(upper, low, high))  1.08 us
  transfers between devices with their start and end apart: 17, of which 7 were waited for; matrix products, arithmetic and copies ran while one was open for 5% of the time, Pallas kernels for 0%

profile of v1, /device:TPU:0, one launch (start us, length us, event | category | flops | bytes accessed | tf_op | source)
XLA Modules:
  0.0 46.9 jit_solution(11910799827125934698)
XLA Ops:
  0.0 1.1 %slice_bitcast_fusion = (f32[128,512]{1,0:T(8,128)S(1)}, f32[128,512]{1,0:T(8,128)S(1)}) fusion(f32[2,128,512]{2,1,0:T(8,128)} %param.6), kind=kLoop, calls=%fused_computation | loop fusion | bytes 1048576 | tf_op jit(solution)/shard_map/squeeze | solution.py:161
  1.1 3.0 %collective-permute-start.15 = (f32[128,512]{1,0:T(8,128)S(1)}, f32[128,512]{1,0:T(8,128)S(1)}, u32[]{:S(2)}, u32[]{:S(2)}) collective-permute-start(f32[128,512]{1,0:T(8,128)S(1)} %get-tuple-element.11.refs_15_), channel_id=1, source_target_pairs={{0,16},{8,24},{16,0},{24,8},{1,17},{9,25},{17,1},{25,9},{2,18},{10... | collective-permute-start | bytes 786440 | tf_op jit(solution)/shard_map/ppermute | solution.py:17
  4.2 1.5 %collective-permute-start.14 = (f32[128,512]{1,0:T(8,128)S(1)}, f32[128,512]{1,0:T(8,128)S(1)}, u32[]{:S(2)}, u32[]{:S(2)}) collective-permute-start(f32[128,512]{1,0:T(8,128)S(1)} %get-tuple-element.11.refs_15_), channel_id=1, source_target_pairs={{0,8},{8,0},{16,24},{24,16},{1,9},{9,1},{17,25},{25,17},{2,10},{10... | collective-permute-start | bytes 786440 | tf_op jit(solution)/shard_map/ppermute | solution.py:17
  5.7 0.5 %collective-permute-start.12 = (f32[128,512]{1,0:T(8,128)S(1)}, f32[128,512]{1,0:T(8,128)S(1)}, u32[]{:S(2)}, u32[]{:S(2)}) collective-permute-start(f32[128,512]{1,0:T(8,128)S(1)} %get-tuple-element.12.refs_11_), channel_id=1, source_target_pairs={{0,16},{8,24},{16,0},{24,8},{1,17},{9,25},{17,1},{25,9},{2,18},{10... | collective-permute-start | bytes 786440 | tf_op jit(solution)/shard_map/ppermute | solution.py:17
  6.2 0.1 collective-permute-start.11
  6.3 1.0 %slice_select_fusion = f32[6,64,128]{2,1,0:T(8,128)S(1)} fusion(f32[6,128,128]{2,1,0:T(8,128)} %bitcast.32, pred[]{:T(512)S(6)} %ne.8), kind=kLoop, calls=%fused_computation.2 | loop fusion | flops 49152 | bytes 589825 | tf_op jit(solution)/shard_map/jit(_where)/select_n | solution.py:31
  7.3 0.1 collective-permute-start
  7.4 0.0 copy-done.1
  7.4 0.6 %fusion.4 = (s32[1]{0:T(128)}, s32[1]{0:T(128)}) fusion(s32[2]{0:T(128)S(1)} %copy-done.1), kind=kLoop, calls=%fused_computation.30 | loop fusion | bytes 16 | tf_op jit(solution)/shard_map/slice | solution.py:164
  11.9 0.0 copy-done.2
  11.9 0.1 dynamic_slice.3
  12.0 0.1 compare_convert_fusion.1
  12.1 0.1 fusion.2
  12.2 0.1 copy.18
  12.4 0.1 copy.19
  12.5 0.1 copy.17
  12.6 0.1 copy.16
  12.7 0.0 collective-permute-done
  12.7 0.0 copy-done
  12.8 2.1 %collective-permute-start.1 = (f32[6,32,128]{2,1,0:T(8,128)S(1)}, f32[6,32,128]{2,1,0:T(8,128)S(1)}, u32[]{:S(2)}, u32[]{:S(2)}) collective-permute-start(f32[6,32,128]{2,1,0:T(8,128)S(1)} %slice_select_fusion.3), channel_id=1, source_target_pairs={{0,2},{1,3},{2,0},{3,1},{4,6},{5,7},{6,4},{7,5},{8,10},{9,11},{10,... | collective-permute-start | bytes 294920 | tf_op jit(solution)/shard_map/ppermute | solution.py:17
  14.8 0.0 collective-permute-done.14.refs_16_
  14.9 0.1 collective-permute-start.6
  15.0 1.1 %collective-permute-done.12.refs_13_ = f32[128,512]{1,0:T(8,128)S(1)} collective-permute-done((f32[128,512]{1,0:T(8,128)S(1)}, f32[128,512]{1,0:T(8,128)S(1)}, u32[]{:S(2)}, u32[]{:S(2)}) %collective-permute-start.12) | collective-permute-done | bytes 262176 | tf_op jit(solution)/shard_map/ppermute | solution.py:17
  16.1 1.7 %collective-permute-start.16 = (f32[128,512]{1,0:T(8,128)S(1)}, f32[128,512]{1,0:T(8,128)S(1)}, u32[]{:S(2)}, u32[]{:S(2)}) collective-permute-start(f32[128,512]{1,0:T(8,128)S(1)} %collective-permute-done.14.refs_16_), channel_id=1, source_target_pairs={{0,16},{8,24},{16,0},{24,8},{1,17},{9,25},{17,1},{25,9},{2,18},{10... | collective-permute-start | bytes 786440 | tf_op jit(solution)/shard_map/ppermute | solution.py:17
  17.8 0.7 %collective-permute-done.1 = f32[6,32,128]{2,1,0:T(8,128)S(1)} collective-permute-done((f32[6,32,128]{2,1,0:T(8,128)S(1)}, f32[6,32,128]{2,1,0:T(8,128)S(1)}, u32[]{:S(2)}, u32[]{:S(2)}) %collective-permute-start.1) | collective-permute-done | bytes 98336 | tf_op jit(solution)/shard_map/ppermute | solution.py:17
  18.5 1.8 %collective-permute-start.13 = (f32[128,512]{1,0:T(8,128)S(1)}, f32[128,512]{1,0:T(8,128)S(1)}, u32[]{:S(2)}, u32[]{:S(2)}) collective-permute-start(f32[128,512]{1,0:T(8,128)S(1)} %collective-permute-done.12.refs_13_), channel_id=1, source_target_pairs={{0,8},{8,0},{16,24},{24,16},{1,9},{9,1},{17,25},{25,17},{2,10},{10... | collective-permute-start | bytes 786440 | tf_op jit(solution)/shard_map/ppermute | solution.py:17
  20.4 0.0 collective-permute-done.6
  20.4 2.8 %collective-permute-start.2 = (f32[6,32,128]{2,1,0:T(8,128)S(1)}, f32[6,32,128]{2,1,0:T(8,128)S(1)}, u32[]{:S(2)}, u32[]{:S(2)}) collective-permute-start(f32[6,32,128]{2,1,0:T(8,128)S(1)} %select_select_fusion.1), channel_id=1, source_target_pairs={{0,4},{1,5},{2,6},{3,7},{4,0},{5,1},{6,2},{7,3},{8,12},{9,13},{10,... | collective-permute-start | bytes 294920 | tf_op jit(solution)/shard_map/ppermute | solution.py:17
  23.2 4.8 %collective-permute-done.2 = f32[6,32,128]{2,1,0:T(8,128)S(1)} collective-permute-done((f32[6,32,128]{2,1,0:T(8,128)S(1)}, f32[6,32,128]{2,1,0:T(8,128)S(1)}, u32[]{:S(2)}, u32[]{:S(2)}) %collective-permute-start.2) | collective-permute-done | bytes 98336 | tf_op jit(solution)/shard_map/ppermute | solution.py:17
  28.0 0.7 %collective-permute-start.7 = (f32[6,32,128]{2,1,0:T(8,128)S(1)}, f32[6,32,128]{2,1,0:T(8,128)S(1)}, u32[]{:S(2)}, u32[]{:S(2)}) collective-permute-start(f32[6,32,128]{2,1,0:T(8,128)S(1)} %select_select_fusion), channel_id=1, source_target_pairs={{0,4},{1,5},{2,6},{3,7},{4,0},{5,1},{6,2},{7,3},{8,12},{9,13},{10,... | collective-permute-start | bytes 294920 | tf_op jit(solution)/shard_map/ppermute | solution.py:17
  28.7 6.7 %collective-permute-done.7 = f32[6,32,128]{2,1,0:T(8,128)S(1)} collective-permute-done((f32[6,32,128]{2,1,0:T(8,128)S(1)}, f32[6,32,128]{2,1,0:T(8,128)S(1)}, u32[]{:S(2)}, u32[]{:S(2)}) %collective-permute-start.7) | collective-permute-done | bytes 98336 | tf_op jit(solution)/shard_map/ppermute | solution.py:17
  35.4 0.0 collective-permute-start.4
  35.4 0.0 collective-permute-done.15.refs_17_
  35.4 0.1 collective-permute-start.3
  35.5 0.0 collective-permute-done.11.refs_12_
  35.5 2.0 %collective-permute-start.8 = (f32[6,32,128]{2,1,0:T(8,128)S(1)}, f32[6,32,128]{2,1,0:T(8,128)S(1)}, u32[]{:S(2)}, u32[]{:S(2)}) collective-permute-start(f32[6,32,128]{2,1,0:T(8,128)S(1)} %broadcast_select_fusion.2.refs_7_), channel_id=1, source_target_pairs={{0,2},{1,3},{2,0},{3,1},{4,6},{5,7},{6,4},{7,5},{8,10},{9,11},{10,... | collective-permute-start | bytes 294920 | tf_op jit(solution)/shard_map/ppermute | solution.py:17
  37.5 0.0 collective-permute-done.4.refs_5_
  37.5 0.0 collective-permute-start.9
  37.5 3.5 %collective-permute-done.3.refs_4_ = f32[6,32,128]{2,1,0:T(8,128)S(1)} collective-permute-done((f32[6,32,128]{2,1,0:T(8,128)S(1)}, f32[6,32,128]{2,1,0:T(8,128)S(1)}, u32[]{:S(2)}, u32[]{:S(2)}) %collective-permute-start.3) | collective-permute-done | bytes 98336 | tf_op jit(solution)/shard_map/ppermute | solution.py:17
  41.0 0.0 collective-permute-start.5
  41.0 1.7 %collective-permute-done.8.refs_8_ = f32[6,32,128]{2,1,0:T(8,128)S(1)} collective-permute-done((f32[6,32,128]{2,1,0:T(8,128)S(1)}, f32[6,32,128]{2,1,0:T(8,128)S(1)}, u32[]{:S(2)}, u32[]{:S(2)}) %collective-permute-start.8) | collective-permute-done | bytes 98336 | tf_op jit(solution)/shard_map/ppermute | solution.py:17
  42.8 0.0 collective-permute-start.10
  42.8 0.0 collective-permute-done.9.refs_9_
  42.8 0.0 collective-permute-done.16.refs_18_
  42.8 0.0 collective-permute-done.13.refs_14_
  42.8 0.0 collective-permute-done.5.refs_6_
  42.8 1.2 %collective-permute-done.10.refs_10_ = f32[6,32,128]{2,1,0:T(8,128)S(1)} collective-permute-done((f32[6,32,128]{2,1,0:T(8,128)S(1)}, f32[6,32,128]{2,1,0:T(8,128)S(1)}, u32[]{:S(2)}, u32[]{:S(2)}) %collective-permute-start.10) | collective-permute-done | bytes 98336 | tf_op jit(solution)/shard_map/ppermute | solution.py:17
  44.1 2.9 %shard_map.55 = f32[768,512]{1,0:T(8,128)} custom-call(s32[2,6,1]{2,1,0:T(8,128)S(1)} %pad_add_fusion.refs_0_, s32[2,6,1]{2,1,0:T(8,128)S(1)} %add_convert_fusion.refs_1_, s32[1]{0:T(128)} %bitcast.8.refs_2_, f32[6,32,128]{2,1,0:T(8,128)S(1)} %broadcast_select_fusion.3.refs_3_, f32[6,32,128]{2,1,0:T(8,128)S(1)} %collective-permute-done.3.refs_4_, ...), custom_call_target="tpu_custom_call" | custom-call | flops 603979776 | bytes 1572864 | tf_op jit(solution)/shard_map/pallas_call | solution.py:131
  (20 shorter events, 0.3 us)
Async XLA Ops:
  0.0 12.7 %copy-start = (f32[1,6,1,128,128]{4,3,2,1,0:T(8,128)S(1)}, f32[1,6,1,128,128]{4,3,2,1,0:T(8,128)}, u32[]{:S(2)}) copy-start(f32[1,6,1,128,128]{4,3,2,1,0:T(8,128)} %param.5) | copy-start | bytes 1179652
  0.0 7.4 %copy-start.1 = (s32[2]{0:T(128)S(1)}, s32[2]{0:T(128)}, u32[]{:S(2)}) copy-start(s32[2]{0:T(128)} %param.7) | copy-start | bytes 28
  0.0 11.9 %copy-start.2 = (s32[2,4]{1,0:T(2,128)S(1)}, s32[2,4]{1,0:T(2,128)}, u32[]{:S(2)}) copy-start(s32[2,4]{1,0:T(2,128)} %param.9) | copy-start | bytes 100
  0.0 11.9 %copy-start.3 = (s32[24]{0:T(128)S(1)}, s32[24]{0:T(128)}, u32[]{:S(2)}) copy-start(s32[24]{0:T(128)} %param.8) | copy-start | bytes 292
  1.1 34.3 %collective-permute-start.15 = (f32[128,512]{1,0:T(8,128)S(1)}, f32[128,512]{1,0:T(8,128)S(1)}, u32[]{:S(2)}, u32[]{:S(2)}) collective-permute-start(f32[128,512]{1,0:T(8,128)S(1)} %get-tuple-element.11.refs_15_), channel_id=1, source_target_pairs={{0,16},{8,24},{16,0},{24,8},{1,17},{9,25},{17,1},{25,9},{2,18},{10... | collective-permute-start | bytes 786440 | tf_op jit(solution)/shard_map/ppermute | solution.py:17
  4.2 10.7 %collective-permute-start.14 = (f32[128,512]{1,0:T(8,128)S(1)}, f32[128,512]{1,0:T(8,128)S(1)}, u32[]{:S(2)}, u32[]{:S(2)}) collective-permute-start(f32[128,512]{1,0:T(8,128)S(1)} %get-tuple-element.11.refs_15_), channel_id=1, source_target_pairs={{0,8},{8,0},{16,24},{24,16},{1,9},{9,1},{17,25},{25,17},{2,10},{10... | collective-permute-start | bytes 786440 | tf_op jit(solution)/shard_map/ppermute | solution.py:17
  5.7 10.4 %collective-permute-start.12 = (f32[128,512]{1,0:T(8,128)S(1)}, f32[128,512]{1,0:T(8,128)S(1)}, u32[]{:S(2)}, u32[]{:S(2)}) collective-permute-start(f32[128,512]{1,0:T(8,128)S(1)} %get-tuple-element.12.refs_11_), channel_id=1, source_target_pairs={{0,16},{8,24},{16,0},{24,8},{1,17},{9,25},{17,1},{25,9},{2,18},{10... | collective-permute-start | bytes 786440 | tf_op jit(solution)/shard_map/ppermute | solution.py:17
  6.2 29.3 %collective-permute-start.11 = (f32[128,512]{1,0:T(8,128)S(1)}, f32[128,512]{1,0:T(8,128)S(1)}, u32[]{:S(2)}, u32[]{:S(2)}) collective-permute-start(f32[128,512]{1,0:T(8,128)S(1)} %get-tuple-element.12.refs_11_), channel_id=1, source_target_pairs={{0,8},{8,0},{16,24},{24,16},{1,9},{9,1},{17,25},{25,17},{2,10},{10... | collective-permute-start | bytes 786440 | tf_op jit(solution)/shard_map/ppermute | solution.py:17
  7.3 5.4 %collective-permute-start = (f32[6,64,128]{2,1,0:T(8,128)S(1)}, f32[6,64,128]{2,1,0:T(8,128)S(1)}, u32[]{:S(2)}, u32[]{:S(2)}) collective-permute-start(f32[6,64,128]{2,1,0:T(8,128)S(1)} %slice_select_fusion), channel_id=1, source_target_pairs={{0,1},{1,0},{2,3},{3,2},{4,5},{5,4},{6,7},{7,6},{8,9},{9,8},{10,11... | collective-permute-start | bytes 589832 | tf_op jit(solution)/shard_map/ppermute | solution.py:17
  12.8 5.7 %collective-permute-start.1 = (f32[6,32,128]{2,1,0:T(8,128)S(1)}, f32[6,32,128]{2,1,0:T(8,128)S(1)}, u32[]{:S(2)}, u32[]{:S(2)}) collective-permute-start(f32[6,32,128]{2,1,0:T(8,128)S(1)} %slice_select_fusion.3), channel_id=1, source_target_pairs={{0,2},{1,3},{2,0},{3,1},{4,6},{5,7},{6,4},{7,5},{8,10},{9,11},{10,... | collective-permute-start | bytes 294920 | tf_op jit(solution)/shard_map/ppermute | solution.py:17
  14.9 5.5 %collective-permute-start.6 = (f32[6,32,128]{2,1,0:T(8,128)S(1)}, f32[6,32,128]{2,1,0:T(8,128)S(1)}, u32[]{:S(2)}, u32[]{:S(2)}) collective-permute-start(f32[6,32,128]{2,1,0:T(8,128)S(1)} %slice_select_fusion.2), channel_id=1, source_target_pairs={{0,2},{1,3},{2,0},{3,1},{4,6},{5,7},{6,4},{7,5},{8,10},{9,11},{10,... | collective-permute-start | bytes 294920 | tf_op jit(solution)/shard_map/ppermute | solution.py:17
  16.1 26.7 %collective-permute-start.16 = (f32[128,512]{1,0:T(8,128)S(1)}, f32[128,512]{1,0:T(8,128)S(1)}, u32[]{:S(2)}, u32[]{:S(2)}) collective-permute-start(f32[128,512]{1,0:T(8,128)S(1)} %collective-permute-done.14.refs_16_), channel_id=1, source_target_pairs={{0,16},{8,24},{16,0},{24,8},{1,17},{9,25},{17,1},{25,9},{2,18},{10... | collective-permute-start | bytes 786440 | tf_op jit(solution)/shard_map/ppermute | solution.py:17
  18.5 24.3 %collective-permute-start.13 = (f32[128,512]{1,0:T(8,128)S(1)}, f32[128,512]{1,0:T(8,128)S(1)}, u32[]{:S(2)}, u32[]{:S(2)}) collective-permute-start(f32[128,512]{1,0:T(8,128)S(1)} %collective-permute-done.12.refs_13_), channel_id=1, source_target_pairs={{0,8},{8,0},{16,24},{24,16},{1,9},{9,1},{17,25},{25,17},{2,10},{10... | collective-permute-start | bytes 786440 | tf_op jit(solution)/shard_map/ppermute | solution.py:17
  20.4 7.6 %collective-permute-start.2 = (f32[6,32,128]{2,1,0:T(8,128)S(1)}, f32[6,32,128]{2,1,0:T(8,128)S(1)}, u32[]{:S(2)}, u32[]{:S(2)}) collective-permute-start(f32[6,32,128]{2,1,0:T(8,128)S(1)} %select_select_fusion.1), channel_id=1, source_target_pairs={{0,4},{1,5},{2,6},{3,7},{4,0},{5,1},{6,2},{7,3},{8,12},{9,13},{10,... | collective-permute-start | bytes 294920 | tf_op jit(solution)/shard_map/ppermute | solution.py:17
  28.0 7.4 %collective-permute-start.7 = (f32[6,32,128]{2,1,0:T(8,128)S(1)}, f32[6,32,128]{2,1,0:T(8,128)S(1)}, u32[]{:S(2)}, u32[]{:S(2)}) collective-permute-start(f32[6,32,128]{2,1,0:T(8,128)S(1)} %select_select_fusion), channel_id=1, source_target_pairs={{0,4},{1,5},{2,6},{3,7},{4,0},{5,1},{6,2},{7,3},{8,12},{9,13},{10,... | collective-permute-start | bytes 294920 | tf_op jit(solution)/shard_map/ppermute | solution.py:17
  35.4 2.1 %collective-permute-start.4 = (f32[6,32,128]{2,1,0:T(8,128)S(1)}, f32[6,32,128]{2,1,0:T(8,128)S(1)}, u32[]{:S(2)}, u32[]{:S(2)}) collective-permute-start(f32[6,32,128]{2,1,0:T(8,128)S(1)} %broadcast_select_fusion.3.refs_3_), channel_id=1, source_target_pairs={{0,1},{1,0},{2,3},{3,2},{4,5},{5,4},{6,7},{7,6},{8,9},{9,8},{10,11... | collective-permute-start | bytes 294920 | tf_op jit(solution)/shard_map/ppermute | solution.py:17
  35.4 5.7 %collective-permute-start.3 = (f32[6,32,128]{2,1,0:T(8,128)S(1)}, f32[6,32,128]{2,1,0:T(8,128)S(1)}, u32[]{:S(2)}, u32[]{:S(2)}) collective-permute-start(f32[6,32,128]{2,1,0:T(8,128)S(1)} %broadcast_select_fusion.3.refs_3_), channel_id=1, source_target_pairs={{0,2},{1,3},{2,0},{3,1},{4,6},{5,7},{6,4},{7,5},{8,10},{9,11},{10,... | collective-permute-start | bytes 294920 | tf_op jit(solution)/shard_map/ppermute | solution.py:17
  35.5 7.3 %collective-permute-start.8 = (f32[6,32,128]{2,1,0:T(8,128)S(1)}, f32[6,32,128]{2,1,0:T(8,128)S(1)}, u32[]{:S(2)}, u32[]{:S(2)}) collective-permute-start(f32[6,32,128]{2,1,0:T(8,128)S(1)} %broadcast_select_fusion.2.refs_7_), channel_id=1, source_target_pairs={{0,2},{1,3},{2,0},{3,1},{4,6},{5,7},{6,4},{7,5},{8,10},{9,11},{10,... | collective-permute-start | bytes 294920 | tf_op jit(solution)/shard_map/ppermute | solution.py:17
  37.5 5.3 %collective-permute-start.9 = (f32[6,32,128]{2,1,0:T(8,128)S(1)}, f32[6,32,128]{2,1,0:T(8,128)S(1)}, u32[]{:S(2)}, u32[]{:S(2)}) collective-permute-start(f32[6,32,128]{2,1,0:T(8,128)S(1)} %broadcast_select_fusion.2.refs_7_), channel_id=1, source_target_pairs={{0,1},{1,0},{2,3},{3,2},{4,5},{5,4},{6,7},{7,6},{8,9},{9,8},{10,11... | collective-permute-start | bytes 294920 | tf_op jit(solution)/shard_map/ppermute | solution.py:17
  41.0 1.8 %collective-permute-start.5 = (f32[6,32,128]{2,1,0:T(8,128)S(1)}, f32[6,32,128]{2,1,0:T(8,128)S(1)}, u32[]{:S(2)}, u32[]{:S(2)}) collective-permute-start(f32[6,32,128]{2,1,0:T(8,128)S(1)} %collective-permute-done.3.refs_4_), channel_id=1, source_target_pairs={{0,1},{1,0},{2,3},{3,2},{4,5},{5,4},{6,7},{7,6},{8,9},{9,8},{10,11... | collective-permute-start | bytes 294920 | tf_op jit(solution)/shard_map/ppermute | solution.py:17
  42.8 1.3 %collective-permute-start.10 = (f32[6,32,128]{2,1,0:T(8,128)S(1)}, f32[6,32,128]{2,1,0:T(8,128)S(1)}, u32[]{:S(2)}, u32[]{:S(2)}) collective-permute-start(f32[6,32,128]{2,1,0:T(8,128)S(1)} %collective-permute-done.8.refs_8_), channel_id=1, source_target_pairs={{0,1},{1,0},{2,3},{3,2},{4,5},{5,4},{6,7},{7,6},{8,9},{9,8},{10,11... | collective-permute-start | bytes 294920 | tf_op jit(solution)/shard_map/ppermute | solution.py:17

commit v2 on v0

v2 whole, which is shorter than its diff:
```python
import functools

import jax
import jax.numpy as jnp
from jax import lax
from jax.experimental import pallas as pl
from jax.experimental.pallas import tpu as pltpu
from jax.sharding import PartitionSpec as P

SMEM = pl.BlockSpec(memory_space=pltpu.SMEM)
VMEM = pl.BlockSpec(memory_space=pltpu.VMEM)
ANY = pl.BlockSpec(memory_space=pl.ANY)
SMALL = pltpu.CompilerParams(vmem_limit_bytes=2 * 1024 * 1024)


def bits_of(count):
    assert count & (count - 1) == 0
    return [1 << place for place in range(count.bit_length() - 1)]


def swap(value, axis, size, bit):
    return lax.ppermute(value, axis, [(i, i ^ bit) for i in range(size)])


def load_kernel(slots, bits, tiles, owner_hbm, occ_hbm, pair_hbm, panel_hbm, blocks_hbm, *refs):
    sections, panel = pair_hbm.shape
    mask_ref, source_ref, piece_ref, panel_ref = refs[:4]
    block_refs, refs = refs[4 : 4 + sections], refs[4 + sections :]
    owner_ref, occ_ref, pair_ref, sems = refs
    sources = [owner_hbm, occ_hbm, pair_hbm, panel_hbm] + [blocks_hbm.at[k] for k in range(sections)]
    targets = [owner_ref, occ_ref, pair_ref, panel_ref, *block_refs]
    copies = [pltpu.make_async_copy(source, target, sems.at[i]) for i, (source, target) in enumerate(zip(sources, targets))]
    for copy in copies:
        copy.start()
    row, col = lax.axis_index("row"), lax.axis_index("col")

    def line(place, value):
        mask_ref[pl.ds(place, 1), :] = jnp.full((1, mask_ref.shape[1]), value, jnp.int32)

    for copy in copies[:3]:
        copy.wait()
    for i, bit in enumerate(bits):
        for k in range(sections):
            line(k * len(bits) + i, jnp.where((owner_ref[k] & bit) == (col & bit), 1, 0))
        line(sections * len(bits) + i, jnp.where((col & bit) != 0, 1, 0))
    for k in range(sections):
        for o in range(tiles):
            label = occ_ref[row * tiles + o]
            count = jnp.int32(0)
            chosen = [jnp.int32(-1)] * slots
            for t in range(panel):
                match = label == pair_ref[k, t]
                chosen = [
                    jnp.where(match & (count == s), row ^ t, place) for s, place in enumerate(chosen)
                ]
                count = count + jnp.where(match, 1, 0)
            for s in range(slots):
                source_ref[k, o * slots + s] = chosen[s]
    number = jnp.int32(0)
    for bit in bits[:-1]:
        number = 2 * number + jnp.where((col & bit) != 0, 1, 0)
    piece_ref[0] = number
    for copy in copies[3:]:
        copy.wait()


def load(owner, occ, pair, panel, integrals, slots, bits):
    sections, depth, columns = integrals.shape
    rows = -(-(sections + 1) * len(bits) // 8) * 8
    shape = jax.ShapeDtypeStruct
    return pl.pallas_call(
        functools.partial(load_kernel, slots, bits, panel.shape[0]),
        out_shape=(
            shape((rows, panel.shape[2]), jnp.int32),
            shape((sections, panel.shape[0] * slots), jnp.int32),
            shape((1,), jnp.int32),
            shape(panel.shape, panel.dtype),
            *[shape((depth, columns), integrals.dtype)] * sections,
        ),
        in_specs=[pl.BlockSpec(memory_space=pltpu.HBM)] * 5,
        out_specs=(VMEM, SMEM, SMEM, VMEM, *[VMEM] * sections),
        scratch_shapes=[
            pltpu.SMEM(owner.shape, jnp.int32),
            pltpu.SMEM(occ.shape, jnp.int32),
            pltpu.SMEM(pair.shape, jnp.int32),
            pltpu.SemaphoreType.DMA((4 + sections,)),
        ],
        compiler_params=pltpu.CompilerParams(vmem_limit_bytes=4 * 1024 * 1024),
    )(*[pltpu.with_memory_space_constraint(x, pltpu.HBM) for x in (owner, occ, pair, panel, integrals)])


def first_kernel(sections, rows, mine_ref, theirs_ref, mask_ref, kept_ref, given_ref):
    half, part = mine_ref.shape[1] // 2, mine_ref.shape[1] // 4
    line = lambda place: mask_ref[pl.ds(place, 1), :][None] != 0
    upper = line(sections * rows)
    cut = lambda ref: jnp.where(upper, ref[:, half:], ref[:, :half])
    mine, theirs = cut(mine_ref), cut(theirs_ref)
    high = line(sections * rows + 1)
    for k in range(sections):
        value = jnp.where(line(k * rows), mine, theirs)
        kept_ref[k] = jnp.where(high, value[:, part:], value[:, :part])
        given_ref[k] = jnp.where(high, value[:, :part], value[:, part:])


def first_choice(panel, other, masks, sections, rows):
    tiles, depth, width = panel.shape
    shape = jax.ShapeDtypeStruct((sections, tiles, depth // 4, width), panel.dtype)
    return pl.pallas_call(
        functools.partial(first_kernel, sections, rows),
        out_shape=[shape] * 2,
        in_specs=[VMEM] * 3,
        out_specs=[VMEM] * 2,
        compiler_params=SMALL,
    )(panel, other, masks)


def next_kernel(sections, rows, place, cut, mask_ref, kept_ref, arrived_ref, *refs):
    line = lambda row: mask_ref[row : row + 1, :][None] != 0
    part = kept_ref.shape[2] // 2
    for k in range(sections):
        value = jnp.where(line(k * rows + place), kept_ref[k], arrived_ref[k])
        if cut:
            high = line(sections * rows + place + 1)
            refs[-2][k] = jnp.where(high, value[:, part:], value[:, :part])
            refs[-1][k] = jnp.where(high, value[:, :part], value[:, part:])
        else:
            refs[-1][k] = value


def next_choice(kept, arrived, masks, rows, place, cut, *after):
    sections, tiles, depth, width = kept.shape
    shape = jax.ShapeDtypeStruct((sections, tiles, depth // (2 if cut else 1), width), kept.dtype)
    out = pl.pallas_call(
        functools.partial(next_kernel, sections, rows, place, cut),
        out_shape=[shape] * (2 if cut else 1),
        in_specs=[VMEM] * 3 + [ANY] * len(after),
        out_specs=[VMEM] * (2 if cut else 1),
        compiler_params=SMALL,
    )(masks, kept, arrived, *after)
    return out if cut else out[0]


def join_kernel(count, *refs):
    parts, out, at = refs[:count], refs[-1], 0
    for part in parts:
        out[at : at + part.shape[0]] = part[...]
        at += part.shape[0]


def join(parts, *after):
    count = sum(part.shape[0] for part in parts)
    return pl.pallas_call(
        functools.partial(join_kernel, len(parts)),
        out_shape=jax.ShapeDtypeStruct((count, *parts[0].shape[1:]), parts[0].dtype),
        in_specs=[VMEM] * len(parts) + [ANY] * len(after),
        out_specs=VMEM,
        compiler_params=SMALL,
    )(*parts, *after)


def split(value):
    high = value.astype(jnp.bfloat16)
    return high, (value - high.astype(jnp.float32)).astype(jnp.bfloat16)


def product(left, right):
    dot = functools.partial(jnp.dot, preferred_element_type=jnp.float32)
    (left_high, left_low), (right_high, right_low) = left, right
    return dot(left_high, right_high) + (dot(left_high, right_low) + dot(left_low, right_high))


def split_kernel(count, *refs):
    for i in range(count):
        refs[count][i], refs[count + 1][i] = split(refs[i][...])


def products_kernel(sections, blocks, sizes, source_ref, piece_ref, high, low, *refs):
    tiles, slots, tile, pieces = sizes
    part_refs, (out_ref, amp, result, sems) = refs[:-4], refs[-4:]
    length, i = tile // pieces, 0
    for part_ref in part_refs:
        for j in range(part_ref.shape[0]):
            start = pl.multiple_of((piece_ref[0] ^ i) * length, length)
            for k in range(sections):
                lanes = pl.ds(k * slots * tile, slots * tile)
                for o in range(tiles):
                    amp[o, pl.ds(start, length), lanes] = part_ref[j, k, o]
            i += 1

    def copy(o):
        return pltpu.make_async_copy(result.at[o], out_ref.at[pl.ds(o * tile, tile)], sems.at[o])

    for o in range(tiles):
        value, left, places = amp[o], [], []
        for k in range(sections):
            for s in range(slots):
                place = source_ref[k, o * slots + s]
                at = (k * slots + s) * tile
                left.append(jnp.where(place >= 0, value[:, at : at + tile], 0.0))
                places.append(k * blocks + jnp.maximum(place, 0))
        pick = lambda ref: jnp.concatenate([ref[place] for place in places], axis=0)
        result[o] = product(split(jnp.concatenate(left, axis=1)), (pick(high), pick(low)))
        copy(o).start()
    for o in range(tiles):
        copy(o).wait()


def products(source, piece, parts, blocks, sizes):
    tiles, slots, tile, pieces = sizes
    sections, count = len(blocks), len(blocks[0])
    columns, depth = blocks[0][0].shape[1], sections * slots * tile
    flat = sum(blocks, [])
    halved = jax.ShapeDtypeStruct((len(flat), tile, columns), jnp.bfloat16)
    high, low = pl.pallas_call(
        functools.partial(split_kernel, len(flat)),
        out_shape=[halved] * 2,
        in_specs=[VMEM] * len(flat),
        out_specs=[VMEM] * 2,
        compiler_params=SMALL,
    )(*flat)
    return pl.pallas_call(
        functools.partial(products_kernel, sections, count, sizes),
        out_shape=jax.ShapeDtypeStruct((tiles * tile, columns), jnp.float32),
        in_specs=[SMEM] * 2 + [VMEM] * (2 + len(parts)),
        out_specs=ANY,
        scratch_shapes=[
            pltpu.VMEM((tiles, tile, depth), jnp.float32),
            pltpu.VMEM((tiles, tile, columns), jnp.float32),
            pltpu.SemaphoreType.DMA((tiles,)),
        ],
        compiler_params=pltpu.CompilerParams(vmem_limit_bytes=16 * 1024 * 1024),
    )(source, piece, high, low, *parts)


def hold(value, *after):
    return join([value], *after)


def on_device(row_size, col_size, amplitudes, integrals, owner_column, occ_irrep, pair_irrep):
    tiles, slots, tile = amplitudes.shape[1:4]
    sections = integrals.shape[0]
    row_bits, col_bits = bits_of(row_size), bits_of(col_size)
    rows = len(col_bits)
    panel = amplitudes[0].transpose(0, 2, 1, 3).reshape(tiles, tile, slots * tile)
    along_row = lambda value, bit: swap(value, "row", row_size, bit)
    along_col = lambda value, bit: swap(value, "col", col_size, bit)

    other = along_col(panel, col_bits[0])
    first = along_row(integrals, row_bits[0])
    masks, source, piece, panel, *own = load(
        owner_column, occ_irrep, pair_irrep, panel, integrals, slots, col_bits
    )
    blocks = [{0: own[k], row_bits[0]: first[k]} for k in range(sections)]
    for k in range(sections):
        blocks[k][row_bits[-1]] = along_row(own[k], row_bits[-1])

    kept, given = first_choice(panel, other, masks, sections, rows)
    for i in range(1, rows - 1):
        cut = i < rows - 2
        out = next_choice(kept, along_col(given, col_bits[i]), masks, rows, i, cut)
        kept, given = out if cut else (out, out)
    for k in range(sections):
        for bit in row_bits[::-1] if k % 2 == 0 else row_bits:
            for offset in list(blocks[k]):
                if offset | bit not in blocks[k]:
                    blocks[k][offset | bit] = along_row(hold(blocks[k][offset], given), bit)
    blocks = [[held[offset] for offset in range(row_size)] for held in blocks]
    after = [blocks[k][row_bits[-1]] for k in range(sections)]
    parts = [next_choice(kept, along_col(given, col_bits[-1]), masks, rows, rows - 1, False, *after)[None]]
    for bit in col_bits[-2::-1]:
        held = parts[0] if len(parts) == 1 else join(parts, *[held[-1] for held in blocks])
        parts.append(along_col(held, bit))
    return products(source, piece, parts, blocks, (tiles, slots, tile, col_size // 2))


def solution(mesh):
    return jax.shard_map(
        functools.partial(on_device, mesh.shape["row"], mesh.shape["col"]),
        mesh=mesh,
        in_specs=(P("col", "row", None, None, None), P(None, "row", "col"), P(), P(), P()),
        out_specs=P("row", "col"),
        check_vma=False,
    )
```

time: 86.4 us -> 33.9 us (0.39)
  waiting for transfers between devices: 56.8 us -> 15.1 us
  between operations: 16.2 us -> 0.07 us
  starting transfers between devices: 0.12 us -> 13.5 us
  local copies, waits for them, and re-layouts: 6.36 us -> 0.03 us
  matrix products: 5.32 us -> 0 us
  Pallas kernels: 0 us -> 5.01 us
  other arithmetic: 1.29 us -> 0 us
    all_gather x2 -> x0, waiting for transfers between devices: 52.7 us -> none  [on_device(): lax.all_gather(integrals[which_section], 'row', axis=0, tiled=True)]
    ppermute x0 -> x10, waiting for transfers between devices: none -> 15.1 us  [swap(): return lax.ppermute(value, axis, [(i, i ^ bit) for i in range(size)])]
    ppermute x0 -> x10, starting transfers between devices: none -> 13.5 us  [swap(): return lax.ppermute(value, axis, [(i, i ^ bit) for i in range(size)])]
    dot_general x2 -> x0, matrix products: 5.32 us -> none  [on_device(): jnp.einsum('osij,osjv->oiv', amp_panel, picked, precision=lax.Precision.H...]
    pallas_call x0 -> x9, Pallas kernels: none -> 5.01 us  [the longest x1 2.69 us: products(): pl.pallas_call(functools.partial(products_kernel, sections, count, sizes)...]
    gather x2 -> x0, local copies, waits for them, and re-layouts: 3.76 us -> none  [on_device(): picked = jnp.take(row_tiles, tile_index, axis=0)]
    psum x1 -> x0, waiting for transfers between devices: 3.43 us -> none  [spread(): return lax.psum(kept, axis)]
    slice x3 -> x0, local copies, waits for them, and re-layouts: 2.5 us -> none  [the longest x1 1.9 us: on_device(): integrals[which_section]]
  transfers between devices with their start and end apart: 3 -> 10, of which waited for: 3 -> 7; matrix products, arithmetic and copies ran while one was open for 7% -> 0% of each run, Pallas kernels for 0% -> 7%
where the time goes in v2:
time: 33.9 us; the launch traced here: 33.7 us
  waiting for transfers between devices  15.1 us (45%)
  starting transfers between devices  13.5 us (40%)
  Pallas kernels  5.01 us (15%)
    ppermute x10, waiting for transfers between devices, swap(): return lax.ppermute(value, axis, [(i, i ^ bit) for i in range(size)])  15.1 us
    ppermute x10, starting transfers between devices, swap(): return lax.ppermute(value, axis, [(i, i ^ bit) for i in range(size)])  13.5 us
    pallas_call x1, Pallas kernels, products(): pl.pallas_call(functools.partial(products_kernel, sections, count, sizes)...  2.69 us
    pallas_call x1, Pallas kernels, load(): pl.pallas_call(functools.partial(load_kernel, slots, bits, panel.shape[0]...  1.8 us
  transfers between devices with their start and end apart: 10, of which 7 were waited for; matrix products, arithmetic and copies ran while one was open for 0% of the time, Pallas kernels for 7%

profile of v2, /device:TPU:0, one launch (start us, length us, event | category | flops | bytes accessed | tf_op | source)
XLA Modules:
  0.0 33.7 jit_solution(15407517382998304260)
XLA Ops:
  0.0 0.5 %collective-permute-start.2 = (f32[6,128,128]{2,1,0:T(8,128)}, f32[6,128,128]{2,1,0:T(8,128)S(1)}, u32[]{:S(2)}, u32[]{:S(2)}) collective-permute-start(f32[6,128,128]{2,1,0:T(8,128)} %bitcast.9), channel_id=1, source_target_pairs={{0,1},{1,0},{2,3},{3,2},{4,5},{5,4},{6,7},{7,6},{8,9},{9,8},{10,11... | collective-permute-start | bytes 1179656 | tf_op jit(solution)/shard_map/ppermute | solution.py:22
  0.5 2.5 %collective-permute-start = (f32[2,128,512]{2,1,0:T(8,128)}, f32[2,128,512]{2,1,0:T(8,128)S(1)}, u32[]{:S(2)}, u32[]{:S(2)}) collective-permute-start(f32[2,128,512]{2,1,0:T(8,128)} %blocks_hbm.1), channel_id=1, source_target_pairs={{0,8},{8,0},{16,24},{24,16},{1,9},{9,1},{17,25},{25,17},{2,10},{10... | collective-permute-start | bytes 1572872 | tf_op jit(solution)/shard_map/ppermute | solution.py:22
  2.9 1.8 %shard_map.55 = (s32[16,128]{1,0:T(8,128)S(1)}, s32[2,6]{1,0:T(2,128)S(1)}, s32[1]{0:T(128)}, f32[6,128,128]{2,1,0:T(8,128)S(1)}, f32[128,512]{1,0:T(8,128)S(1)}, /*index=5*/f32[128,512]{1,0:T(8,128)S(1)}) custom-call(s32[2]{0:T(128)} %owner_hbm.1, s32[24]{0:T(128)} %occ_hbm.1, s32[2,4]{1,0:T(2,128)} %pair_hbm.1, f32[6,128,128]{2,1,0:T(8,128)} %bitcast.10, ...), custom_call_target="tpu_custom_call" | custom-call | tf_op jit(solution)/shard_map/pallas_call | solution.py:71
  4.8 0.0 collective-permute-done.2.theirs_ref
  4.8 0.1 shard_map.56
  4.8 1.6 %collective-permute-start.3 = (f32[2,6,32,128]{3,2,1,0:T(8,128)S(1)}, f32[2,6,32,128]{3,2,1,0:T(8,128)S(1)}, u32[]{:S(2)}, u32[]{:S(2)}) collective-permute-start(f32[2,6,32,128]{3,2,1,0:T(8,128)S(1)} %get-tuple-element.21), channel_id=1, source_target_pairs={{0,2},{1,3},{2,0},{3,1},{4,6},{5,7},{6,4},{7,5},{8,10},{9,11},{10,... | collective-permute-start | bytes 589832 | tf_op jit(solution)/shard_map/ppermute | solution.py:22
  6.5 1.5 %collective-permute-start.5 = (f32[128,512]{1,0:T(8,128)S(1)}, f32[128,512]{1,0:T(8,128)S(1)}, u32[]{:S(2)}, u32[]{:S(2)}) collective-permute-start(f32[128,512]{1,0:T(8,128)S(1)} %get-tuple-element.22.refs_4_), channel_id=1, source_target_pairs={{0,16},{8,24},{16,0},{24,8},{1,17},{9,25},{17,1},{25,9},{2,18},{10... | collective-permute-start | bytes 786440 | tf_op jit(solution)/shard_map/ppermute | solution.py:22
  8.0 0.5 %collective-permute-start.1 = (f32[128,512]{1,0:T(8,128)S(1)}, f32[128,512]{1,0:T(8,128)S(1)}, u32[]{:S(2)}, u32[]{:S(2)}) collective-permute-start(f32[128,512]{1,0:T(8,128)S(1)} %get-tuple-element.17.refs_0_), channel_id=1, source_target_pairs={{0,16},{8,24},{16,0},{24,8},{1,17},{9,25},{17,1},{25,9},{2,18},{10... | collective-permute-start | bytes 786440 | tf_op jit(solution)/shard_map/ppermute | solution.py:22
  8.5 3.4 %collective-permute-done.3.arrived_ref = f32[2,6,32,128]{3,2,1,0:T(8,128)S(1)} collective-permute-done((f32[2,6,32,128]{3,2,1,0:T(8,128)S(1)}, f32[2,6,32,128]{3,2,1,0:T(8,128)S(1)}, u32[]{:S(2)}, u32[]{:S(2)}) %collective-permute-start.3) | collective-permute-done | bytes 196640 | tf_op jit(solution)/shard_map/ppermute | solution.py:22
  12.0 2.7 %collective-permute-start.7 = (f32[2,6,32,128]{3,2,1,0:T(8,128)S(1)}, f32[2,6,32,128]{3,2,1,0:T(8,128)S(1)}, u32[]{:S(2)}, u32[]{:S(2)}) collective-permute-start(f32[2,6,32,128]{3,2,1,0:T(8,128)S(1)} %shard_map.57.refs_1_.kept_ref), channel_id=1, source_target_pairs={{0,4},{1,5},{2,6},{3,7},{4,0},{5,1},{6,2},{7,3},{8,12},{9,13},{10,... | collective-permute-start | bytes 589832 | tf_op jit(solution)/shard_map/ppermute | solution.py:22
  14.6 1.1 %collective-permute-done = f32[2,128,512]{2,1,0:T(8,128)S(1)} collective-permute-done((f32[2,128,512]{2,1,0:T(8,128)}, f32[2,128,512]{2,1,0:T(8,128)S(1)}, u32[]{:S(2)}, u32[]{:S(2)}) %collective-permute-start) | collective-permute-done | bytes 524320 | tf_op jit(solution)/shard_map/ppermute | solution.py:22
  15.8 1.8 %collective-permute-start.4 = (f32[128,512]{1,0:T(8,128)S(1)}, f32[128,512]{1,0:T(8,128)S(1)}, u32[]{:S(2)}, u32[]{:S(2)}) collective-permute-start(f32[128,512]{1,0:T(8,128)S(1)} %shard_map.58), channel_id=1, source_target_pairs={{0,16},{8,24},{16,0},{24,8},{1,17},{9,25},{17,1},{25,9},{2,18},{10... | collective-permute-start | bytes 786440 | tf_op jit(solution)/shard_map/ppermute | solution.py:22
  17.6 0.0 collective-permute-done.5.refs_0_.refs_6_.refs_1_
  17.7 1.6 %collective-permute-start.6 = (f32[128,512]{1,0:T(8,128)S(1)}, f32[128,512]{1,0:T(8,128)S(1)}, u32[]{:S(2)}, u32[]{:S(2)}) collective-permute-start(f32[128,512]{1,0:T(8,128)S(1)} %shard_map.59), channel_id=1, source_target_pairs={{0,8},{8,0},{16,24},{24,16},{1,9},{9,1},{17,25},{25,17},{2,10},{10... | collective-permute-start | bytes 786440 | tf_op jit(solution)/shard_map/ppermute | solution.py:22
  19.2 2.0 %collective-permute-done.1.refs_2_.refs_0_ = f32[128,512]{1,0:T(8,128)S(1)} collective-permute-done((f32[128,512]{1,0:T(8,128)S(1)}, f32[128,512]{1,0:T(8,128)S(1)}, u32[]{:S(2)}, u32[]{:S(2)}) %collective-permute-start.1) | collective-permute-done | bytes 262176 | tf_op jit(solution)/shard_map/ppermute | solution.py:22
  21.3 2.1 %collective-permute-done.7.arrived_ref = f32[2,6,32,128]{3,2,1,0:T(8,128)S(1)} collective-permute-done((f32[2,6,32,128]{3,2,1,0:T(8,128)S(1)}, f32[2,6,32,128]{3,2,1,0:T(8,128)S(1)}, u32[]{:S(2)}, u32[]{:S(2)}) %collective-permute-start.7) | collective-permute-done | bytes 196640 | tf_op jit(solution)/shard_map/ppermute | solution.py:22
  23.4 0.7 %collective-permute-start.8 = (f32[1,2,6,32,128]{4,3,2,1,0:T(8,128)S(1)}, f32[1,2,6,32,128]{4,3,2,1,0:T(8,128)S(1)}, u32[]{:S(2)}, u32[]{:S(2)}) collective-permute-start(f32[1,2,6,32,128]{4,3,2,1,0:T(8,128)S(1)} %bitcast.6), channel_id=1, source_target_pairs={{0,2},{1,3},{2,0},{3,1},{4,6},{5,7},{6,4},{7,5},{8,10},{9,11},{10,... | collective-permute-start | bytes 589832 | tf_op jit(solution)/shard_map/ppermute | solution.py:22
  24.1 1.8 %collective-permute-done.4.refs_3_.refs_2_ = f32[128,512]{1,0:T(8,128)S(1)} collective-permute-done((f32[128,512]{1,0:T(8,128)S(1)}, f32[128,512]{1,0:T(8,128)S(1)}, u32[]{:S(2)}, u32[]{:S(2)}) %collective-permute-start.4) | collective-permute-done | bytes 262176 | tf_op jit(solution)/shard_map/ppermute | solution.py:22
  25.9 0.0 collective-permute-done.6.refs_7_.refs_3_
  25.9 3.3 %collective-permute-done.8.refs_1_ = f32[1,2,6,32,128]{4,3,2,1,0:T(8,128)S(1)} collective-permute-done((f32[1,2,6,32,128]{4,3,2,1,0:T(8,128)S(1)}, f32[1,2,6,32,128]{4,3,2,1,0:T(8,128)S(1)}, u32[]{:S(2)}, u32[]{:S(2)}) %collective-permute-start.8) | collective-permute-done | bytes 196640 | tf_op jit(solution)/shard_map/ppermute | solution.py:22
  29.2 0.1 collective-permute-start.9
  29.3 0.3 %shard_map.60 = (bf16[8,128,512]{2,1,0:T(8,128)(2,1)S(1)}, bf16[8,128,512]{2,1,0:T(8,128)(2,1)S(1)}) custom-call(f32[128,512]{1,0:T(8,128)S(1)} %get-tuple-element.17.refs_0_, f32[128,512]{1,0:T(8,128)S(1)} %get-tuple-element.26.refs_0_.refs_1_, f32[128,512]{1,0:T(8,128)S(1)} %collective-permute-done.1.refs_2_.refs_0_, ...), custom_call_target="tpu_custom_call" | custom-call | tf_op jit(solution)/shard_map/pallas_call | solution.py:214
  29.7 1.4 %collective-permute-done.9.refs_2_ = f32[2,2,6,32,128]{4,3,2,1,0:T(8,128)S(1)} collective-permute-done((f32[2,2,6,32,128]{4,3,2,1,0:T(8,128)S(1)}, f32[2,2,6,32,128]{4,3,2,1,0:T(8,128)S(1)}, u32[]{:S(2)}, u32[]{:S(2)}) %collective-permute-start.9) | collective-permute-done | bytes 393248 | tf_op jit(solution)/shard_map/ppermute | solution.py:22
  31.0 2.7 %shard_map.63 = f32[768,512]{1,0:T(8,128)} custom-call(s32[2,6]{1,0:T(2,128)S(1)} %get-tuple-element.15.source_ref, s32[1]{0:T(128)} %get-tuple-element.16.piece_ref, bf16[8,128,512]{2,1,0:T(8,128)(2,1)S(1)} %get-tuple-element.23.high, bf16[8,128,512]{2,1,0:T(8,128)(2,1)S(1)} %get-tuple-element.24.low, f32[1,2,6,32,128]{4,3,2,1,0:T(8,128)S(1)} %bitcast.8, ...), custom_call_target="tpu_custom_call" | custom-call | tf_op jit(solution)/shard_map/pallas_call | solution.py:221
  (6 shorter events, 0.1 us)
Async XLA Ops:
  0.0 4.8 %collective-permute-start.2 = (f32[6,128,128]{2,1,0:T(8,128)}, f32[6,128,128]{2,1,0:T(8,128)S(1)}, u32[]{:S(2)}, u32[]{:S(2)}) collective-permute-start(f32[6,128,128]{2,1,0:T(8,128)} %bitcast.9), channel_id=1, source_target_pairs={{0,1},{1,0},{2,3},{3,2},{4,5},{5,4},{6,7},{7,6},{8,9},{9,8},{10,11... | collective-permute-start | bytes 1179656 | tf_op jit(solution)/shard_map/ppermute | solution.py:22
  0.5 15.3 %collective-permute-start = (f32[2,128,512]{2,1,0:T(8,128)}, f32[2,128,512]{2,1,0:T(8,128)S(1)}, u32[]{:S(2)}, u32[]{:S(2)}) collective-permute-start(f32[2,128,512]{2,1,0:T(8,128)} %blocks_hbm.1), channel_id=1, source_target_pairs={{0,8},{8,0},{16,24},{24,16},{1,9},{9,1},{17,25},{25,17},{2,10},{10... | collective-permute-start | bytes 1572872 | tf_op jit(solution)/shard_map/ppermute | solution.py:22
  4.8 7.1 %collective-permute-start.3 = (f32[2,6,32,128]{3,2,1,0:T(8,128)S(1)}, f32[2,6,32,128]{3,2,1,0:T(8,128)S(1)}, u32[]{:S(2)}, u32[]{:S(2)}) collective-permute-start(f32[2,6,32,128]{3,2,1,0:T(8,128)S(1)} %get-tuple-element.21), channel_id=1, source_target_pairs={{0,2},{1,3},{2,0},{3,1},{4,6},{5,7},{6,4},{7,5},{8,10},{9,11},{10,... | collective-permute-start | bytes 589832 | tf_op jit(solution)/shard_map/ppermute | solution.py:22
  6.5 11.2 %collective-permute-start.5 = (f32[128,512]{1,0:T(8,128)S(1)}, f32[128,512]{1,0:T(8,128)S(1)}, u32[]{:S(2)}, u32[]{:S(2)}) collective-permute-start(f32[128,512]{1,0:T(8,128)S(1)} %get-tuple-element.22.refs_4_), channel_id=1, source_target_pairs={{0,16},{8,24},{16,0},{24,8},{1,17},{9,25},{17,1},{25,9},{2,18},{10... | collective-permute-start | bytes 786440 | tf_op jit(solution)/shard_map/ppermute | solution.py:22
  8.0 13.3 %collective-permute-start.1 = (f32[128,512]{1,0:T(8,128)S(1)}, f32[128,512]{1,0:T(8,128)S(1)}, u32[]{:S(2)}, u32[]{:S(2)}) collective-permute-start(f32[128,512]{1,0:T(8,128)S(1)} %get-tuple-element.17.refs_0_), channel_id=1, source_target_pairs={{0,16},{8,24},{16,0},{24,8},{1,17},{9,25},{17,1},{25,9},{2,18},{10... | collective-permute-start | bytes 786440 | tf_op jit(solution)/shard_map/ppermute | solution.py:22
  12.0 11.4 %collective-permute-start.7 = (f32[2,6,32,128]{3,2,1,0:T(8,128)S(1)}, f32[2,6,32,128]{3,2,1,0:T(8,128)S(1)}, u32[]{:S(2)}, u32[]{:S(2)}) collective-permute-start(f32[2,6,32,128]{3,2,1,0:T(8,128)S(1)} %shard_map.57.refs_1_.kept_ref), channel_id=1, source_target_pairs={{0,4},{1,5},{2,6},{3,7},{4,0},{5,1},{6,2},{7,3},{8,12},{9,13},{10,... | collective-permute-start | bytes 589832 | tf_op jit(solution)/shard_map/ppermute | solution.py:22
  15.8 10.1 %collective-permute-start.4 = (f32[128,512]{1,0:T(8,128)S(1)}, f32[128,512]{1,0:T(8,128)S(1)}, u32[]{:S(2)}, u32[]{:S(2)}) collective-permute-start(f32[128,512]{1,0:T(8,128)S(1)} %shard_map.58), channel_id=1, source_target_pairs={{0,16},{8,24},{16,0},{24,8},{1,17},{9,25},{17,1},{25,9},{2,18},{10... | collective-permute-start | bytes 786440 | tf_op jit(solution)/shard_map/ppermute | solution.py:22
  17.7 8.2 %collective-permute-start.6 = (f32[128,512]{1,0:T(8,128)S(1)}, f32[128,512]{1,0:T(8,128)S(1)}, u32[]{:S(2)}, u32[]{:S(2)}) collective-permute-start(f32[128,512]{1,0:T(8,128)S(1)} %shard_map.59), channel_id=1, source_target_pairs={{0,8},{8,0},{16,24},{24,16},{1,9},{9,1},{17,25},{25,17},{2,10},{10... | collective-permute-start | bytes 786440 | tf_op jit(solution)/shard_map/ppermute | solution.py:22
  23.4 5.8 %collective-permute-start.8 = (f32[1,2,6,32,128]{4,3,2,1,0:T(8,128)S(1)}, f32[1,2,6,32,128]{4,3,2,1,0:T(8,128)S(1)}, u32[]{:S(2)}, u32[]{:S(2)}) collective-permute-start(f32[1,2,6,32,128]{4,3,2,1,0:T(8,128)S(1)} %bitcast.6), channel_id=1, source_target_pairs={{0,2},{1,3},{2,0},{3,1},{4,6},{5,7},{6,4},{7,5},{8,10},{9,11},{10,... | collective-permute-start | bytes 589832 | tf_op jit(solution)/shard_map/ppermute | solution.py:22
  29.2 1.8 %collective-permute-start.9 = (f32[2,2,6,32,128]{4,3,2,1,0:T(8,128)S(1)}, f32[2,2,6,32,128]{4,3,2,1,0:T(8,128)S(1)}, u32[]{:S(2)}, u32[]{:S(2)}) collective-permute-start(f32[2,2,6,32,128]{4,3,2,1,0:T(8,128)S(1)} %shard_map.62), channel_id=1, source_target_pairs={{0,1},{1,0},{2,3},{3,2},{4,5},{5,4},{6,7},{7,6},{8,9},{9,8},{10,11... | collective-permute-start | bytes 1179656 | tf_op jit(solution)/shard_map/ppermute | solution.py:22
